TPU v7x, 32 devices: a whole 2x2x4 slice. The times are simulated.
32 devices in a mesh: dp: 8 (over z, y), reg: 4 (over x, core).
Axes of the slice: x: 2, y: 2, z: 4, core: 2. Of those that a mesh axis runs over, the one named last changes fastest.
Arguments:
- tokens: bfloat16 [30720, 768], P(('dp', 'reg')), may hold values from -6 to 6
- cotangent: bfloat16 [30720, 768], P(('dp', 'reg')), may hold values from -6 to 6
- distance_cot: float32 [160], P('dp'), may hold values from -262144 to 262144
- lengths: int32 [160, 2], P('dp'), may hold values from 16 to 128, as said below
- w_qkv: bfloat16 [768, 2304], replicated, may hold values from -0.21875 to 0.21875
- q_bias: float32 [768], replicated, may hold values from -3 to 3
- v_bias: float32 [768], replicated, may hold values from -3 to 3
- w_out: bfloat16 [768, 768], replicated, may hold values from -0.875 to 0.875
- out_bias: float32 [768], replicated, may hold values from -3 to 3
- ln1_gain: float32 [768], replicated, may hold values from 0.1 to 1.9
- ln1_bias: float32 [768], replicated, may hold values from -3 to 3
- w_in: bfloat16 [768, 3072], replicated, may hold values from -0.21875 to 0.21875
- in_bias: float32 [3072], replicated, may hold values from -3 to 3
- w_down: bfloat16 [3072, 768], replicated, may hold values from -0.109375 to 0.109375
- down_bias: float32 [768], replicated, may hold values from -3 to 3
- ln2_gain: float32 [768], replicated, may hold values from 0.1 to 1.9
- ln2_bias: float32 [768], replicated, may hold values from -3 to 3
Outputs:
- layer_out: bfloat16 [30720, 768], P(('dp', 'reg'))
- distance: float32 [160], P(('dp', 'reg'))
- tokens_grad: float32 [30720, 768], P(('dp', 'reg'))
- w_qkv_grad: float32 [768, 2304], replicated
- q_bias_grad: float32 [768], replicated
- v_bias_grad: float32 [768], replicated
- w_out_grad: float32 [768, 768], replicated
- out_bias_grad: float32 [768], replicated
- ln1_gain_grad: float32 [768], replicated
- ln1_bias_grad: float32 [768], replicated
- w_in_grad: float32 [768, 3072], replicated
- in_bias_grad: float32 [3072], replicated
- w_down_grad: float32 [3072, 768], replicated
- down_bias_grad: float32 [768], replicated
- ln2_gain_grad: float32 [768], replicated
- ln2_bias_grad: float32 [768], replicated
Inputs may be any that keep to these rules, and one draw needn't show every extreme that they name: `lengths`: column 0 is a pair's word count, 16 to 64; column 1 its region count, 32 to 128. Each aligned block of 20 pairs holds a pair with 64 words and 128 regions.
All inputs are finite; a program needn't handle non-finite values.
Results may differ from a plain program's by a relative error of at most 0.015.
The roundings to bfloat16 on the way count: a program that leaves them out, or rounds other values in their place, can miss the bound.
Values may be sent and summed in bfloat16 or wider, within the bound.
A program may use at most 320 MiB of HBM per device.

v0:
```python
from functools import partial

import jax
import jax.numpy as jnp
from jax import lax
from jax.sharding import PartitionSpec as P

D = 768
HEADS = 12
HEAD_DIM = 64
WORDS = 64
REGIONS = 128
ITERS = 50


BETA = 0.5
EPS = 1e-06
HIGH = lax.Precision.HIGHEST


def layer_norm(hidden, gain, shift):
    center = hidden - jnp.mean(hidden, -1, keepdims=True)
    scaled = center * lax.rsqrt(jnp.mean(center * center, -1, keepdims=True) + EPS)
    return scaled * gain + shift


def cost_pieces(joint_mask, word_rows, region_rows):
    word_unit = word_rows * lax.rsqrt(jnp.sum(word_rows * word_rows, -1, keepdims=True) + EPS)
    region_unit = region_rows * lax.rsqrt(
        jnp.sum(region_rows * region_rows, -1, keepdims=True) + EPS
    )
    cosine = jnp.einsum("pwd,prd->pwr", word_unit, region_unit, precision=HIGH)
    cost_tile = (1.0 - cosine) * joint_mask
    return (cost_tile, jnp.exp(-cost_tile / BETA) * joint_mask)


def half_first(region_valid, region_len, kernel, transport, word_scale):
    joined = kernel * transport
    region_tot = jnp.sum(joined * word_scale[:, :, None], 1)
    region_scale = region_valid / (region_len[:, None] * region_tot + (1.0 - region_valid))
    partial_sum = jnp.sum(joined * region_scale[:, None, :], 2)
    return (joined, region_scale, partial_sum)


def half_second(word_valid, word_len, joined, region_scale, word_tot):
    word_scale = word_valid / (word_len[:, None] * word_tot + (1.0 - word_valid))
    transport = joined * region_scale[:, None, :] * word_scale[:, :, None]
    return (transport, word_scale)


def word_total(partial_sum):
    return lax.psum(partial_sum, "reg")


def word_total_back(grad_total):
    return lax.psum(grad_total, "reg")


def outer_rows(left_in, right_in):
    return lax.dot_general(
        left_in, right_in, (((0,), (0,)), ((), ())), preferred_element_type=jnp.float32
    )


def back_dot(grad_in, weight_in):
    return lax.dot_general(
        grad_in, weight_in, (((1,), (1,)), ((), ())), preferred_element_type=jnp.float32
    )


def on_device(
    tokens,
    cotangent,
    distance_cot,
    lengths,
    w_qkv,
    q_bias,
    v_bias,
    w_out,
    out_bias,
    ln1_gain,
    ln1_bias,
    w_in,
    in_bias,
    w_down,
    down_bias,
    ln2_gain,
    ln2_bias,
):
    slot_rows = WORDS + REGIONS
    local_pairs = tokens.shape[0] // slot_rows
    local_rows = local_pairs * slot_rows
    reg_index = lax.axis_index("reg")
    score_scale = HEAD_DIM ** (-0.5)
    own_lengths = lax.dynamic_slice_in_dim(lengths, reg_index * local_pairs, local_pairs, 0)
    position = jnp.arange(slot_rows)[None, :]
    key_valid = jnp.where(
        position < WORDS, position < own_lengths[:, 0:1], position - WORDS < own_lengths[:, 1:2]
    )
    bias_full = jnp.concatenate([q_bias, jnp.zeros_like(q_bias), v_bias])
    packed = (jnp.dot(tokens, w_qkv, preferred_element_type=jnp.float32) + bias_full).astype(
        jnp.bfloat16
    )
    split_heads = packed.reshape(local_pairs, slot_rows, 3, HEADS, HEAD_DIM)
    queries = split_heads[:, :, 0]
    keys_all = split_heads[:, :, 1]
    values = split_heads[:, :, 2]

    def make_scores():
        raw_scores = (
            jnp.einsum("pqhd,pkhd->phqk", queries, keys_all, preferred_element_type=jnp.float32)
            * score_scale
        )
        return jnp.where(key_valid[:, None, None, :], raw_scores, -1e30)

    scores = make_scores()
    row_top = jnp.max(scores, -1, keepdims=True)
    exponent = jnp.exp(scores - row_top)
    row_total = jnp.sum(exponent, -1, keepdims=True)
    probs = exponent / row_total
    log_total = row_top + jnp.log(row_total)
    context = jnp.einsum(
        "phqk,pkhd->pqhd", probs.astype(jnp.bfloat16), values, preferred_element_type=jnp.float32
    )
    context = context.reshape(local_rows, D).astype(jnp.bfloat16)
    attended = jnp.dot(context, w_out, preferred_element_type=jnp.float32) + out_bias
    first_sum = tokens.astype(jnp.float32) + attended
    normed, first_back = jax.vjp(layer_norm, first_sum, ln1_gain, ln1_bias)
    normed_low = normed.astype(jnp.bfloat16)
    inner = jnp.dot(normed_low, w_in, preferred_element_type=jnp.float32) + in_bias
    activated, gelu_back = jax.vjp(partial(jax.nn.gelu, approximate=False), inner)
    activated_low = activated.astype(jnp.bfloat16)
    branch = jnp.dot(activated_low, w_down, preferred_element_type=jnp.float32) + down_bias
    result, second_back = jax.vjp(layer_norm, normed + branch, ln2_gain, ln2_bias)
    result_low = result.astype(jnp.bfloat16)
    gathered = lax.all_gather(result_low, "reg", axis=0, tiled=True)
    gathered = gathered.reshape(lengths.shape[0], slot_rows, D).astype(jnp.float32)
    columns = REGIONS // lax.axis_size("reg")
    first_col = reg_index * columns
    pair_count = gathered.shape[0]
    word_rows = gathered[:, :WORDS]
    region_rows = lax.dynamic_slice_in_dim(gathered, WORDS + first_col, columns, 1)
    word_len = lengths[:, 0].astype(jnp.float32)
    region_len = lengths[:, 1].astype(jnp.float32)
    word_valid = (jnp.arange(WORDS)[None, :] < lengths[:, 0:1]).astype(jnp.float32)
    region_valid = ((first_col + jnp.arange(columns))[None, :] < lengths[:, 1:2]).astype(
        jnp.float32
    )
    joint_mask = word_valid[:, :, None] * region_valid[:, None, :]
    (cost_tile, kernel), cost_back = jax.vjp(
        partial(cost_pieces, joint_mask), word_rows, region_rows
    )
    first_part = partial(half_first, region_valid, region_len)
    second_part = partial(half_second, word_valid, word_len)

    def forward_step(state_in, unused_item):
        transport_in, scale_in = state_in
        joined, region_scale, partial_sum = first_part(kernel, transport_in, scale_in)
        word_tot = word_total(partial_sum)
        return (second_part(joined, region_scale, word_tot), (transport_in, scale_in, word_tot))

    start_scale = word_valid / word_len[:, None]
    (transport, word_scale), history = lax.scan(
        forward_step, (joint_mask, start_scale), None, length=ITERS
    )
    distance_part = jnp.sum(transport * cost_tile, (1, 2))
    distance = lax.psum_scatter(distance_part, "reg", scatter_dimension=0, tiled=True)

    def backward_step(state_in, saved):
        grad_transport, grad_scale, grad_kernel = state_in
        transport_in, scale_in, word_tot = saved
        (joined, region_scale, unused_sum), first_vjp = jax.vjp(
            first_part, kernel, transport_in, scale_in
        )
        unused_pair, second_vjp = jax.vjp(second_part, joined, region_scale, word_tot)
        grad_joined, grad_region, grad_total = second_vjp((grad_transport, grad_scale))
        grad_partial = word_total_back(grad_total)
        more_kernel, grad_prev, grad_scale_prev = first_vjp(
            (grad_joined, grad_region, grad_partial)
        )
        return ((grad_prev, grad_scale_prev, grad_kernel + more_kernel), None)

    start_back = (
        distance_cot[:, None, None] * cost_tile,
        jnp.zeros_like(word_scale),
        jnp.zeros_like(kernel),
    )
    (unused_plan, unused_scale, grad_kernel), unused_out = lax.scan(
        backward_step, start_back, history, reverse=True
    )
    grad_words, grad_regions = cost_back((distance_cot[:, None, None] * transport, grad_kernel))
    grad_group = jnp.concatenate([grad_words, jnp.zeros((pair_count, REGIONS, D), jnp.float32)], 1)
    grad_group = lax.dynamic_update_slice_in_dim(grad_group, grad_regions, WORDS + first_col, 1)
    grad_group = grad_group.reshape(pair_count * slot_rows, D)
    grad_rows = lax.psum_scatter(
        grad_group.astype(jnp.bfloat16), "reg", scatter_dimension=0, tiled=True
    ).astype(jnp.float32)
    grad_result = cotangent.astype(jnp.float32) + grad_rows
    grad_second, grad_gain2, grad_shift2 = second_back(grad_result)
    grad_branch = grad_second.astype(jnp.bfloat16)
    grad_w_down = outer_rows(activated_low, grad_branch)
    grad_down_bias = jnp.sum(grad_branch.astype(jnp.float32), 0)
    (grad_inner,) = gelu_back(back_dot(grad_branch, w_down))
    grad_inner = grad_inner.astype(jnp.bfloat16)
    grad_w_in = outer_rows(normed_low, grad_inner)
    grad_in_bias = jnp.sum(grad_inner.astype(jnp.float32), 0)
    grad_normed = grad_second + back_dot(grad_inner, w_in)
    grad_first, grad_gain1, grad_shift1 = first_back(grad_normed)
    grad_attended = grad_first.astype(jnp.bfloat16)
    grad_w_out = outer_rows(context, grad_attended)
    grad_out_bias = jnp.sum(grad_attended.astype(jnp.float32), 0)
    grad_context = (
        back_dot(grad_attended, w_out)
        .astype(jnp.bfloat16)
        .reshape(local_pairs, slot_rows, HEADS, HEAD_DIM)
    )
    probs_again = jnp.exp(make_scores() - log_total)
    grad_probs = jnp.einsum(
        "pqhd,pkhd->phqk", grad_context, values, preferred_element_type=jnp.float32
    )
    grad_values = jnp.einsum(
        "phqk,pqhd->pkhd",
        probs_again.astype(jnp.bfloat16),
        grad_context,
        preferred_element_type=jnp.float32,
    )
    grad_scores = probs_again * (grad_probs - jnp.sum(grad_probs * probs_again, -1, keepdims=True))
    grad_scores = grad_scores.astype(jnp.bfloat16)
    grad_queries = (
        jnp.einsum("phqk,pkhd->pqhd", grad_scores, keys_all, preferred_element_type=jnp.float32)
        * score_scale
    )
    grad_keys = (
        jnp.einsum("phqk,pqhd->pkhd", grad_scores, queries, preferred_element_type=jnp.float32)
        * score_scale
    )
    grad_packed = (
        jnp.stack([grad_queries, grad_keys, grad_values], 2)
        .reshape(local_rows, 3 * D)
        .astype(jnp.bfloat16)
    )
    grad_w_qkv = outer_rows(tokens, grad_packed)
    grad_bias_sum = jnp.sum(grad_packed.astype(jnp.float32), 0)
    grad_q_bias = grad_bias_sum[:D]
    grad_v_bias = grad_bias_sum[2 * D :]
    grad_tokens = grad_first + back_dot(grad_packed, w_qkv)
    gradients = (
        grad_w_qkv,
        grad_q_bias,
        grad_v_bias,
        grad_w_out,
        grad_out_bias,
        grad_gain1,
        grad_shift1,
        grad_w_in,
        grad_in_bias,
        grad_w_down,
        grad_down_bias,
        grad_gain2,
        grad_shift2,
    )
    flat_grads = jnp.concatenate([member.reshape(-1) for member in gradients])
    device_count = lax.axis_size(("dp", "reg"))
    block_len = device_count * 128
    padded_len = -(-flat_grads.shape[0] // block_len) * block_len
    per_device = padded_len // device_count
    spread = jnp.pad(flat_grads, (0, padded_len - flat_grads.shape[0])).reshape(
        per_device, device_count
    )
    grad_table = jnp.transpose(spread).reshape(padded_len // 128, 128)
    shared = lax.psum_scatter(grad_table, ("dp", "reg"), scatter_dimension=0, tiled=True)
    summed = lax.all_gather(shared.astype(jnp.bfloat16), ("dp", "reg"), axis=0, tiled=True).astype(
        shared.dtype
    )
    summed = jnp.transpose(summed.reshape(device_count, per_device)).reshape(-1)
    outputs = []
    offset = 0
    for member in gradients:
        outputs.append(summed[offset : offset + member.size].reshape(member.shape))
        offset = offset + member.size
    return (
        result_low,
        distance,
        grad_tokens,
        outputs[0],
        outputs[1],
        outputs[2],
        outputs[3],
        outputs[4],
        outputs[5],
        outputs[6],
        outputs[7],
        outputs[8],
        outputs[9],
        outputs[10],
        outputs[11],
        outputs[12],
    )


def solution(mesh):
    return jax.shard_map(
        on_device,
        mesh=mesh,
        in_specs=(
            P(("dp", "reg"), None),
            P(("dp", "reg"), None),
            P("dp"),
            P("dp", None),
            P(),
            P(),
            P(),
            P(),
            P(),
            P(),
            P(),
            P(),
            P(),
            P(),
            P(),
            P(),
            P(),
        ),
        out_specs=(
            P(("dp", "reg"), None),
            P(("dp", "reg")),
            P(("dp", "reg"), None),
            P(),
            P(),
            P(),
            P(),
            P(),
            P(),
            P(),
            P(),
            P(),
            P(),
            P(),
            P(),
            P(),
        ),
        check_vma=False,
    )
```

profile of v0, /device:TPU:0, one launch (start us, length us, event | category | flops | bytes accessed | tf_op | source)
XLA Modules:
  0.0 3796.9 jit_solution(475472982923340790)
XLA Ops:
  16.1 14.1 reshape.433
  83.5 34.0 multiply_convert_fusion.1
  140.4 33.2 all-gather.4.cloned.1.call-done
  193.0 1043.2 %while.38 = (s32[]{:T(128)}, f32[20,64,32]{2,1,0:T(8,128)}, f32[20,64]{1,0:T(8,128)S(1)}, f32[50,20,64,32]{3,2,1,0:T(8,128)}, f32[50,20,64]{2,1,0:T(8,128)}, /*i...) while((s32[]{:T(128)}, f32[20,64,32]{2,1,0:T(8,128)}, ...), condition=%wide.region_12.13_spmd.clone, body=%wide.region_8.12_spmd.clone.sunk | while | flops 297602 | bytes 3050633 | solution.py:163
  1236.9 1261.0 %while.39 = (s32[]{:T(128)}, f32[20,64,32]{2,1,0:T(8,128)}, f32[20,64]{1,0:T(8,128)}, f32[20,64,32]{2,1,0:T(8,128)}, f32[20]{0:T(128)}, /*index=5*/f32[50,20,64]...) while((s32[]{:T(128)}, f32[20,64,32]{2,1,0:T(8,128)}, ...), condition=%wide.region_22.23_spmd.clone, body=%wide.region_15.22_spmd.clone.sunk | while | flops 932484 | bytes 2950327 | solution.py:188
  2526.5 55.6 %reduce-scatter.4.cloned.1.call-done = bf16[960,768]{1,0:T(8,128)(2,1)} async-done(((bf16[3840,768]{1,0:T(8,128)(2,1)}), bf16[960,768]{1,0:T(8,128)(2,1)}) %reduce-scatter.4.cloned.1.call-update) | async-done | bytes 1474576 | tf_op jit(solution)/shard_map/reduce_scatter | solution.py:195
  2590.4 17.9 convert_reduce_fusion
  2663.7 13.9 multiply_reduce_fusion.7
  2731.8 13.3 convert_element_type.139
  2778.3 21.3 dynamic-update-slice.3
  2803.5 80.6 %dynamic-update-slice.7 = f32[7087104]{0:T(1024)} dynamic-update-slice(f32[7087104]{0:T(1024)} %constant_dynamic-update-slice_fusion.4, f32[2359296]{0:T(1024)} %bitcast.146, s32[]{} %constant.211) | dynamic-update-slice | bytes 18874372
  2885.5 80.3 %dynamic-update-slice.9 = f32[7087104]{0:T(1024)} dynamic-update-slice(f32[7087104]{0:T(1024)} %constant_dynamic-update-slice_fusion.3, f32[2359296]{0:T(1024)} %reshape.418, s32[]{} %constant.213) | dynamic-update-slice | bytes 18874372
  2969.8 20.8 pad.5
  2990.5 66.8 %reshape.419 = f32[221568,32]{1,0:T(8,128)} reshape(f32[7090176]{0:T(1024)} %pad.5) | data formatting | bytes 56721408 | tf_op jit(solution)/shard_map/reshape | solution.py:267
  3057.3 66.9 %copy.154 = f32[32,221568]{1,0:T(8,128)} copy(f32[32,221568]{0,1:T(8,128)} %bitcast.19) | data formatting | bytes 56721408 | tf_op jit(solution)/shard_map/transpose | solution.py:270
  3124.2 25.4 reshape.420
  3149.6 303.3 %fusion.8 = f32[1744,128]{1,0:T(8,128)} fusion(f32[55392,128]{1,0:T(8,128)} %reshape.420), kind=kCustom, calls=%all-reduce-scatter | all-reduce-scatter fusion | flops 7143425 | bytes 29253632
  3486.1 91.3 %all-gather.6.cloned.1.call-done = bf16[32,1731,128]{2,1,0:T(8,128)(2,1)} async-done(((bf16[1,1731,128]{2,1,0:T(8,128)(2,1)}), bf16[32,1731,128]{2,1,0:T(8,128)(2,1)}) %all-gather.6.cloned.1.call-update) | async-done | bytes 14180368 | tf_op jit(solution)/shard_map/all_gather | solution.py:272
  3659.3 16.1 copy.155
  3675.4 19.3 reshape.422
  3694.7 21.0 copy.164
  3715.7 25.8 reshape.425
  3741.5 21.0 copy.162
  3762.5 27.7 reshape.424
  (1856 shorter events, 2706.8 us)
Async XLA Ops:
  7.2 166.4 %all-gather.4.cloned.1.call-start = ((), (), s32[]{:S(2)}) async-start(), calls=%async_computation.1 | async-start | bytes 7372800 | tf_op jit(solution)/shard_map/all_gather | solution.py:136
  78.0 39.5 %slice-start.6 = ((s8[4718592]{0:T(1024)(128)(4,1)}), s8[4194304]{0:T(1024)(128)(4,1)S(1)}, s32[]{:S(2)}) async-start(s8[4718592]{0:T(1024)(128)(4,1)} %bitcast.151), calls=%async_computation.10 | async-start | bytes 8388608
  82.0 35.5 copy-start.8
  83.4 34.1 copy-start.26
  83.5 34.1 slice-start.7
  83.5 34.1 copy-start.75
  126.6 2455.6 %reduce-scatter.4.cloned.1.call-start = ((), (), s32[]{:S(2)}) async-start(), calls=%async_computation.2 | async-start | bytes 7372800 | tf_op jit(solution)/shard_map/reduce_scatter | solution.py:195
  2524.5 57.7 %copy-start.42 = (f32[960]{0:T(1024)S(1)}, f32[960]{0:T(1024)}, u32[]{:S(2)}) copy-start(f32[960]{0:T(1024)} %copy-done.41) | copy-start | bytes 11524
  2524.5 57.7 %copy-start.46 = (f32[960]{0:T(1024)S(1)}, f32[960]{0:T(1024)}, u32[]{:S(2)}) copy-start(f32[960]{0:T(1024)} %copy-done.45) | copy-start | bytes 11524
  2524.5 62.5 %copy-start.54 = (f32[960]{0:T(1024)S(1)}, f32[960]{0:T(1024)}, u32[]{:S(2)}) copy-start(f32[960]{0:T(1024)} %copy-done.53) | copy-start | bytes 11524
  2524.5 1052.9 %all-gather.6.cloned.1.call-start = ((), (), s32[]{:S(2)}) async-start(), calls=%async_computation.3 | async-start | bytes 14665728 | tf_op jit(solution)/shard_map/all_gather | solution.py:272
  2654.5 23.1 slice-start
  2654.5 23.1 slice-start.1
  2775.7 23.9 copy-start.63
  2775.7 25.2 copy-start.67
  2775.7 26.5 copy-start.66
  2803.5 80.6 %copy-start.64 = (f32[3072]{0:T(1024)S(1)}, f32[3072]{0:T(1024)}, u32[]{:S(2)}) copy-start(f32[3072]{0:T(1024)} %get-tuple-element.585) | copy-start | bytes 36868
  2885.5 80.4 %copy-start.62 = (f32[768]{0:T(1024)S(1)}, f32[768]{0:T(1024)}, u32[]{:S(2)}) copy-start(f32[768]{0:T(1024)} %get-tuple-element.583) | copy-start | bytes 9220
  2885.5 81.7 %copy-start.61 = (f32[768]{0:T(1024)S(1)}, f32[768]{0:T(1024)}, u32[]{:S(2)}) copy-start(f32[768]{0:T(1024)} %get-tuple-element.523) | copy-start | bytes 9220
  2885.5 83.0 %copy-start.60 = (f32[768]{0:T(1024)S(1)}, f32[768]{0:T(1024)}, u32[]{:S(2)}) copy-start(f32[768]{0:T(1024)} %get-tuple-element.527) | copy-start | bytes 9220
  3149.6 316.6 %copy-start.76 = (u32[32]{0:T(128)S(1)}, u32[32]{0:T(128)}, u32[]{:S(2)}) copy-start(u32[32]{0:T(128)} %constant.199) | copy-start | bytes 388
  3149.6 317.8 %copy-start.70 = (f32[20]{0:T(128)S(1)}, f32[20]{0:T(128)}, u32[]{:S(2)}) copy-start(f32[20]{0:T(128)} %get-tuple-element.614) | copy-start | bytes 244
  3149.6 327.6 %copy-start.59 = (f32[960]{0:T(1024)S(1)}, f32[960]{0:T(1024)}, u32[]{:S(2)}) copy-start(f32[960]{0:T(1024)} %copy-done.58) | copy-start | bytes 11524
  3454.5 4.9 collective-permute-start
  (362 other events, 914.3 us)
Sparse Core Ops, SparseCore 0:
  126.7 46.8 all-gather.3
  2524.6 57.5 reduce-scatter.3
  3466.3 111.0 all-gather.5
where the time goes:
time: 3850 us; the launch traced here: 3800 us
  blocking collectives  1410 us (37%)
  local copies, waits for them, and re-layouts  1040 us (27%)
  other arithmetic  954 us (25%)
  waiting for transfers between devices  181 us (5%)
  matrix products  174 us (5%)
    psum x50, blocking collectives, word_total_back(): return lax.psum(grad_total, 'reg')  565 us
    psum x50, blocking collectives, word_total(): return lax.psum(partial_sum, 'reg')  536 us
    unnamed x2, blocking collectives  312 us
    unnamed x189, local copies, waits for them, and re-layouts  265 us
    dynamic_update_slice x150, local copies, waits for them, and re-layouts, on_device(): lax.scan(forward_step, (joint_mask, start_scale), None, length=ITERS)  195 us
    add x50, other arithmetic, backward_step(): return ((grad_prev, grad_scale_prev, grad_kernel + more_kernel), None)  189 us
    reduce_sum x100, other arithmetic, half_first(): region_tot = jnp.sum(joined * word_scale[:, :, None], 1)  156 us
    slice x27, local copies, waits for them, and re-layouts, on_device(): outputs.append(summed[offset:offset + member.size].reshape(member.shape))  112 us
  transfers between devices with their start and end apart: 4, of which 4 were waited for; matrix products, arithmetic and copies ran while one was open for 0% of the time, Pallas kernels for 0%

commit v1 on v0

v1 whole, which is shorter than its diff:
```python
import functools
import heapq
import math

import jax
import jax.numpy as jnp
from jax import lax
from jax.experimental import pallas as pl
from jax.experimental.pallas import tpu as pltpu
from jax.sharding import PartitionSpec as P

D = 768
HEADS = 12
HEAD_DIM = 64
WORDS = 64
REGIONS = 128
SLOT = WORDS + REGIONS
ITERS = 50
EPS = 1e-06
f32 = jnp.float32
bf16 = jnp.bfloat16
MESH = pl.DeviceIdType.MESH
VMEM_LIMIT = 60 * 2**20

BLK = 1536
COLS = 256
NBLK = 18
HALVES = 5
RBLK = BLK - (BLK >> HALVES)
ORDERS = (
    ("c", "x", "y", "z0", "z1"),
    ("c", "y", "x", "z0", "z1"),
    ("c", "z0", "x", "y", "z1"),
    ("c", "x", "y", "z0", "z1"),
    ("c", "y", "x", "z0", "z1"),
    ("c", "z0", "y", "x", "z1"),
)


def order_of(block):
    return ORDERS[block % len(ORDERS)]


def event_order(ready, extra, rate=85e3, core_rate=470e3, delay=1.8, cost=0.25):
    free = {}
    heap = [(at, block - 1000, block, -1) for block, at in enumerate(ready)]
    heapq.heapify(heap)
    found = []
    count = 0
    last = 2 * HALVES + extra - 1
    while heap:
        now, _, block, event = heapq.heappop(heap)
        if event >= 0:
            found.append((now, block, event))
            now = now + cost
        if event == last:
            continue
        step = event + 1
        if step < HALVES:
            dim, size = order_of(block)[step], BLK >> (step + 1)
        elif step < HALVES + extra:
            dim, size = "far", BLK >> HALVES
        else:
            back = last - step
            dim, size = order_of(block)[back], BLK >> (back + 1)
        sent = size * COLS * 2
        line = "z" if dim in ("z0", "z1") else dim
        took = sent / core_rate if dim == "c" else 2 * sent / rate
        begin = max(now, free.get(line, 0.0))
        free[line] = begin + took
        more = took if dim == "z1" else 0.0
        heapq.heappush(heap, (begin + took + more + delay, count, block, step))
        count += 1
    return found


def mesh_partners(ndp):
    dp = lax.axis_index("dp")
    reg = lax.axis_index("reg")
    names = [("c", "reg", 1), ("x", "reg", 2), ("y", "dp", 1), ("z0", "dp", 2), ("z1", "dp", 4)]
    step = 8
    while step < ndp:
        names.append(("far%d" % step, "dp", step))
        step *= 2
    partners = {}
    for name, axis, step in names:
        at = reg if axis == "reg" else dp
        bit = lax.rem(at // step, 2)
        other = at + step - 2 * step * bit
        partners[name] = (bit, (dp, other) if axis == "reg" else (other, reg))
    return partners


class Exchange:
    def __init__(self, ndp, table, full, landing, far, small, small_in, sems):
        self.partners = mesh_partners(ndp)
        self.fars = [name for name in self.partners if name.startswith("far")]
        self.extra = len(self.fars)
        self.table, self.full, self.landing, self.far = table, full, landing, far
        self.small, self.small_in = small, small_in
        self.rs_send, self.rs_recv, self.ag_send, self.ag_recv, self.far_send, self.far_recv, self.sm_send, self.sm_recv, self.own = sems

    def barrier(self):
        bar = pltpu.get_barrier_semaphore()
        for _, who in self.partners.values():
            pl.semaphore_signal(bar, inc=1, device_id=who, device_id_type=MESH)
        pl.semaphore_wait(bar, len(self.partners))

    def offset(self, block, steps):
        at, size = block * BLK, BLK
        for step in range(steps):
            size //= 2
            at = at + self.partners[order_of(block)[step]][0] * size
        return pl.multiple_of(at, 16) if steps else at

    def halving(self, block, step):
        bit, who = self.partners[order_of(block)[step]]
        size = BLK >> (step + 1)
        src = pl.multiple_of(self.offset(block, step) + (1 - bit) * size, 16)
        land = block * RBLK + (BLK - (BLK >> step))
        return pltpu.make_async_remote_copy(
            self.table.at[pl.ds(src, size)],
            self.landing.at[pl.ds(land, size)],
            self.rs_send.at[block, step],
            self.rs_recv.at[block, step],
            device_id=who,
            device_id_type=MESH,
        )

    def far_step(self, block, index):
        _, who = self.partners[self.fars[index]]
        size = BLK >> HALVES
        src = self.offset(block, HALVES)
        return pltpu.make_async_remote_copy(
            self.table.at[pl.ds(src, size)],
            self.far.at[block, index],
            self.far_send.at[block, index],
            self.far_recv.at[block, index],
            device_id=who,
            device_id_type=MESH,
        )

    def returning(self, block, step):
        _, who = self.partners[order_of(block)[step]]
        size = BLK >> (step + 1)
        src = self.offset(block, step + 1)
        held = self.table if step + 1 == HALVES else self.full
        return pltpu.make_async_remote_copy(
            held.at[pl.ds(src, size)],
            self.full.at[pl.ds(src, size)],
            self.ag_send.at[block, step],
            self.ag_recv.at[block, step],
            device_id=who,
            device_id_type=MESH,
        )

    def keep(self, block):
        at = pl.ds(self.offset(block, HALVES), BLK >> HALVES)
        return pltpu.make_async_copy(self.table.at[at], self.full.at[at], self.own.at[block])

    def produce(self, block):
        self.halving(block, 0).start()

    def start_after(self, block, event):
        step = event + 1
        if step < HALVES:
            self.halving(block, step).start()
        elif step < HALVES + self.extra:
            self.far_step(block, step - HALVES).start()
        elif step < 2 * HALVES + self.extra:
            back = 2 * HALVES + self.extra - 1 - step
            if back + 1 == HALVES:
                self.keep(block).start()
            self.returning(block, back).start()

    def handle(self, block, event):
        if event < HALVES:
            self.halving(block, event).wait_recv()
            size = BLK >> (event + 1)
            off = self.offset(block, event + 1)
            land = block * RBLK + (BLK - (BLK >> event))
            rows = min(size, 192)

            def add(index, carry):
                at = pl.ds(pl.multiple_of(off + index * rows, 16), rows)
                come = self.landing[pl.ds(pl.multiple_of(land + index * rows, 16), rows), :]
                self.table[at, :] = (self.table[at, :].astype(f32) + come.astype(f32)).astype(bf16)
                return carry

            lax.fori_loop(0, size // rows, add, 0)
        elif event < HALVES + self.extra:
            index = event - HALVES
            copy = self.far_step(block, index)
            copy.wait()
            at = pl.ds(self.offset(block, HALVES), BLK >> HALVES)
            self.table[at, :] = (self.table[at, :].astype(f32) + self.far[block, index].astype(f32)).astype(bf16)
        else:
            back = 2 * HALVES + self.extra - 1 - event
            self.returning(block, back).wait_recv()
            if back + 1 == HALVES:
                self.keep(block).wait()
        self.start_after(block, event)

    def small_copy(self, index):
        _, who = self.partners[list(self.partners)[index]]
        return pltpu.make_async_remote_copy(
            self.small,
            self.small_in.at[index],
            self.sm_send.at[index],
            self.sm_recv.at[index],
            device_id=who,
            device_id_type=MESH,
        )

    def small_handle(self, index):
        self.small_copy(index).wait()
        self.small[...] = self.small[...] + self.small_in[index]
        if index + 1 < len(self.partners):
            self.small_copy(index + 1).start()

    def finish(self):
        for block in range(NBLK):
            for step in range(HALVES):
                self.halving(block, step).wait_send()
                self.returning(block, step).wait_send()


def exchange_scratch(ndp):
    extra = max(int(math.log2(ndp)) - 3, 0)
    count = HALVES + extra
    dma = pltpu.SemaphoreType.DMA
    return [
        pltpu.VMEM((NBLK * RBLK, COLS), bf16),
        pltpu.VMEM((NBLK, max(extra, 1), BLK >> HALVES, COLS), bf16),
        pltpu.VMEM((16, D), f32),
        pltpu.VMEM((count, 16, D), f32),
        dma((NBLK, HALVES)),
        dma((NBLK, HALVES)),
        dma((NBLK, HALVES)),
        dma((NBLK, HALVES)),
        dma((NBLK, max(extra, 1))),
        dma((NBLK, max(extra, 1))),
        dma((count,)),
        dma((count,)),
        dma((NBLK,)),
    ]


def sum_table(table, small, ndp):
    extra = max(int(math.log2(ndp)) - 3, 0)
    events = event_order([0.05 * block for block in range(NBLK)], extra)

    def kernel(table_in, small_ref, table_out, small_out, gbuf, lsem, landing, far, sbuf, sland, *sems):
        ex = Exchange(ndp, gbuf, table_out, landing, far, sbuf, sland, sems)
        rows = [pl.ds(block * BLK, BLK) for block in range(NBLK)]
        loads = [pltpu.make_async_copy(table_in.at[at], gbuf.at[at], lsem.at[b]) for b, at in enumerate(rows)]
        for load in loads:
            load.start()
        sbuf[...] = small_ref[...]
        ex.barrier()
        ex.small_copy(0).start()
        for block in range(NBLK):
            loads[block].wait()
            ex.produce(block)
        for index in range(len(ex.partners)):
            ex.small_handle(index)
        small_out[...] = sbuf[...]
        for _, block, event in events:
            ex.handle(block, event)
        ex.finish()

    anywhere = pl.BlockSpec(memory_space=pl.ANY)
    vmem = pl.BlockSpec(memory_space=pltpu.VMEM)
    dma = pltpu.SemaphoreType.DMA
    return pl.pallas_call(
        kernel,
        out_shape=(jax.ShapeDtypeStruct((NBLK * BLK, COLS), bf16), jax.ShapeDtypeStruct((16, D), f32)),
        in_specs=[anywhere, vmem],
        out_specs=(anywhere, vmem),
        scratch_shapes=[pltpu.VMEM((NBLK * BLK, COLS), bf16), dma((NBLK,))] + exchange_scratch(ndp),
        compiler_params=pltpu.CompilerParams(collective_id=1, has_side_effects=True, vmem_limit_bytes=VMEM_LIMIT),
        name="sum_table",
    )(table, small)


def widen(table, rows, grid, in_map, out_map, shape):
    def kernel(a, o):
        o[...] = a[...].astype(f32)

    return pl.pallas_call(
        kernel,
        grid=grid,
        out_shape=jax.ShapeDtypeStruct(shape, f32),
        in_specs=[pl.BlockSpec((rows, COLS), in_map)],
        out_specs=pl.BlockSpec((rows, COLS), out_map),
        name="widen",
    )(table)


def unpack_table(table):
    down = widen(table, 512, (6, 3), lambda j, c: (6 * j + c, 0), lambda j, c: (j, c), (4 * D, D))
    w_in = widen(table, 768, (6, 2), lambda j, c: (4 * j + 2 + c, 0), lambda j, c: (0, 2 * j + c), (D, 4 * D))
    out = widen(table, 768, (3,), lambda c: (24 + c, 0), lambda c: (0, c), (D, D))
    qkv = widen(table, 768, (9,), lambda c: (27 + c, 0), lambda c: (0, c), (D, 3 * D))
    return qkv, out, w_in, down


def pack_table(qkv, out, w_in, down):
    down = down.astype(bf16).reshape(6, 512, 3, 256).transpose(0, 2, 1, 3).reshape(6, 1, BLK, COLS)
    w_in = w_in.astype(bf16).reshape(768, 6, 2, 256).transpose(1, 2, 0, 3).reshape(6, 1, BLK, COLS)
    first = jnp.concatenate([down, w_in], 1).reshape(12 * BLK, COLS)
    tail = jnp.concatenate([out, qkv], 1).astype(bf16).reshape(768, 6, 2, 256).transpose(1, 2, 0, 3)
    return jnp.concatenate([first, tail.reshape(6 * BLK, COLS)], 0)


def align_body(pairs, first, rows_ref, len_ref, dcot_ref, grad_ref, dist_ref, kern, trans, uhist, ahist, acc, alpha, gamma, cosr):
    P = range(pairs)
    eye = lax.broadcasted_iota(jnp.int32, (REGIONS, REGIONS), 0) == lax.broadcasted_iota(jnp.int32, (REGIONS, REGIONS), 1)
    wcol = lax.broadcasted_iota(jnp.int32, (WORDS, 1), 0)
    rrow = lax.broadcasted_iota(jnp.int32, (1, REGIONS), 1)
    nlen = [len_ref[first + p, 0] for p in P]
    mlen = [len_ref[first + p, 1] for p in P]
    nf = [v.astype(f32) for v in nlen]
    mf = [v.astype(f32) for v in mlen]
    dc = [dcot_ref[first + p] for p in P]
    wv = [(wcol < nlen[p]).astype(f32) for p in P]
    rv = [(rrow < mlen[p]).astype(f32) for p in P]
    rxs, rys = [], []
    for p in P:
        x = rows_ref[SLOT * p:SLOT * p + WORDS, :]
        y = rows_ref[SLOT * p + WORDS:SLOT * (p + 1), :]
        xf, yf = x.astype(f32), y.astype(f32)
        rx = lax.rsqrt(jnp.sum(xf * xf, -1, keepdims=True) + EPS)
        ry = lax.rsqrt(jnp.sum(yf * yf, -1, keepdims=True) + EPS)
        ryr = jnp.sum(jnp.where(eye, ry, 0.0), 0, keepdims=True)
        rxs.append(rx); rys.append((ry, ryr))
        cos = lax.dot_general(x, y, (((1,), (1,)), ((), ())), preferred_element_type=f32) * rx * ryr
        joint = wv[p] * rv[p]
        cost = (1.0 - cos) * joint
        cosr[p] = cos
        kern[p] = jnp.exp(-2.0 * cost) * joint
        trans[p] = joint
        ahist[0, p] = jnp.broadcast_to(wv[p] / nf[p], (WORDS, REGIONS))
    def fwd(t, _):
        joined = [kern[p] * trans[p] for p in P]
        a = [ahist[t, p] for p in P]
        s = [jnp.sum(joined[p] * a[p], 0, keepdims=True) for p in P]
        b = [rv[p] / (mf[p] * s[p] + (1.0 - rv[p])) for p in P]
        u = [joined[p] * b[p] for p in P]
        w = [jnp.sum(u[p], 1, keepdims=True) for p in P]
        an = [wv[p] / (nf[p] * w[p] + (1.0 - wv[p])) for p in P]
        for p in P:
            uhist[t, p] = u[p]
            ahist[t + 1, p] = jnp.broadcast_to(an[p], (WORDS, REGIONS))
            trans[p] = u[p] * an[p]
        return 0
    lax.fori_loop(0, ITERS, fwd, 0)
    cols = []
    for p in P:
        joint = wv[p] * rv[p]
        cost = (1.0 - cosr[p]) * joint
        tc = trans[p] * cost
        dist_ref[p] = jnp.sum(tc)
        g = tc * dc[p]
        cols.append(jnp.sum(g, 0, keepdims=True))
        alpha[p] = jnp.broadcast_to(jnp.sum(g, 1, keepdims=True), (WORDS, REGIONS))
        gamma[p] = jnp.zeros((WORDS, REGIONS), f32)
        acc[p] = float(ITERS) * g
    def bwd(i, cols):
        t = ITERS - i
        tf = t.astype(f32)
        u = [uhist[t - 1, p] for p in P]
        x = [nf[p] * alpha[p] * ahist[t, p] for p in P]
        y = [mf[p] * ahist[t - 1, p] for p in P]
        beta = [cols[p] - jnp.sum(u[p] * x[p], 0, keepdims=True) for p in P]
        ub = [u[p] * beta[p] for p in P]
        gm = [-y[p] * jnp.sum(ub[p], 1, keepdims=True) for p in P]
        go = [gamma[p] for p in P]
        ac = [acc[p] for p in P]
        for p in P:
            acc[p] = ac[p] - tf * (u[p] * x[p] + y[p] * ub[p])
            alpha[p] = 2.0 * gm[p] - go[p]
            gamma[p] = gm[p]
        return tuple(jnp.zeros_like(c) for c in cols)
    lax.fori_loop(0, ITERS, bwd, tuple(cols))
    for p in P:
        x = rows_ref[SLOT * p:SLOT * p + WORDS, :]
        y = rows_ref[SLOT * p + WORDS:SLOT * (p + 1), :]
        rx = rxs[p]; ry, ryr = rys[p]
        gc = dc[p] * trans[p] - 2.0 * acc[p]
        gcos = gc * cosr[p]
        m = gc * rx * ryr
        hi = m.astype(bf16)
        lo = (m - hi.astype(f32)).astype(bf16)
        nt = (((1,), (0,)), ((), ())); tn = (((0,), (0,)), ((), ()))
        gx = lax.dot_general(hi, y, nt, preferred_element_type=f32) + lax.dot_general(lo, y, nt, preferred_element_type=f32)
        gy = lax.dot_general(hi, x, tn, preferred_element_type=f32) + lax.dot_general(lo, x, tn, preferred_element_type=f32)
        sx = rx * rx * jnp.sum(gcos, 1, keepdims=True)
        sy = ry * ry * jnp.sum(jnp.where(eye, jnp.sum(gcos, 0, keepdims=True), 0.0), 1, keepdims=True)
        grad_ref[SLOT * p:SLOT * p + WORDS, :] = sx * x.astype(f32) - gx
        grad_ref[SLOT * p + WORDS:SLOT * (p + 1), :] = sy * y.astype(f32) - gy

def scratch(pairs):
    v = lambda *s: pltpu.VMEM(s, f32)
    W = (WORDS, REGIONS)
    return [v(pairs, *W), v(pairs, *W), v(ITERS, pairs, *W), v(ITERS + 1, pairs, *W), v(pairs, *W), v(pairs, *W), v(pairs, *W), v(pairs, *W)]

def align(rows, lengths, dcot, first, interpret=False):
    pairs = rows.shape[0] // SLOT
    def k(rows_ref, len_ref, dcot_ref, grad_ref, dist_ref, *sc):
        align_body(pairs, first(), rows_ref, len_ref, dcot_ref, grad_ref, dist_ref, *sc)
    V = pl.BlockSpec(memory_space=pltpu.VMEM); S = pl.BlockSpec(memory_space=pltpu.SMEM)
    return pl.pallas_call(k, out_shape=(jax.ShapeDtypeStruct((pairs * SLOT, D), f32), jax.ShapeDtypeStruct((pairs,), f32)),
        in_specs=[V, S, S], out_specs=(V, S), scratch_shapes=scratch(pairs), interpret=interpret,
        compiler_params=pltpu.CompilerParams(vmem_limit_bytes=60 * 2**20))(rows, lengths, dcot)


def layer_norm(hidden, gain, shift):
    center = hidden - jnp.mean(hidden, -1, keepdims=True)
    scaled = center * lax.rsqrt(jnp.mean(center * center, -1, keepdims=True) + EPS)
    return scaled * gain + shift


def outer_rows(left_in, right_in):
    return lax.dot_general(left_in, right_in, (((0,), (0,)), ((), ())), preferred_element_type=jnp.float32)


def back_dot(grad_in, weight_in):
    return lax.dot_general(grad_in, weight_in, (((1,), (1,)), ((), ())), preferred_element_type=jnp.float32)


def on_device(ndp, tokens, cotangent, distance_cot, lengths, w_qkv, q_bias, v_bias, w_out, out_bias, ln1_gain, ln1_bias, w_in, in_bias, w_down, down_bias, ln2_gain, ln2_bias):
    slot_rows = SLOT
    local_pairs = tokens.shape[0] // slot_rows
    local_rows = local_pairs * slot_rows
    reg_index = lax.axis_index("reg")
    score_scale = HEAD_DIM ** (-0.5)
    own_lengths = lax.dynamic_slice_in_dim(lengths, reg_index * local_pairs, local_pairs, 0)
    position = jnp.arange(slot_rows)[None, :]
    key_valid = jnp.where(position < WORDS, position < own_lengths[:, 0:1], position - WORDS < own_lengths[:, 1:2])
    bias_full = jnp.concatenate([q_bias, jnp.zeros_like(q_bias), v_bias])
    packed = (jnp.dot(tokens, w_qkv, preferred_element_type=jnp.float32) + bias_full).astype(jnp.bfloat16)
    split_heads = packed.reshape(local_pairs, slot_rows, 3, HEADS, HEAD_DIM)
    queries = split_heads[:, :, 0]
    keys_all = split_heads[:, :, 1]
    values = split_heads[:, :, 2]

    def make_scores():
        raw_scores = jnp.einsum("pqhd,pkhd->phqk", queries, keys_all, preferred_element_type=jnp.float32) * score_scale
        return jnp.where(key_valid[:, None, None, :], raw_scores, -1e30)

    scores = make_scores()
    row_top = jnp.max(scores, -1, keepdims=True)
    exponent = jnp.exp(scores - row_top)
    row_total = jnp.sum(exponent, -1, keepdims=True)
    probs = exponent / row_total
    log_total = row_top + jnp.log(row_total)
    context = jnp.einsum("phqk,pkhd->pqhd", probs.astype(jnp.bfloat16), values, preferred_element_type=jnp.float32)
    context = context.reshape(local_rows, D).astype(jnp.bfloat16)
    attended = jnp.dot(context, w_out, preferred_element_type=jnp.float32) + out_bias
    first_sum = tokens.astype(jnp.float32) + attended
    normed, first_back = jax.vjp(layer_norm, first_sum, ln1_gain, ln1_bias)
    normed_low = normed.astype(jnp.bfloat16)
    inner = jnp.dot(normed_low, w_in, preferred_element_type=jnp.float32) + in_bias
    activated, gelu_back = jax.vjp(functools.partial(jax.nn.gelu, approximate=False), inner)
    activated_low = activated.astype(jnp.bfloat16)
    branch = jnp.dot(activated_low, w_down, preferred_element_type=jnp.float32) + down_bias
    result, second_back = jax.vjp(layer_norm, normed + branch, ln2_gain, ln2_bias)
    result_low = result.astype(jnp.bfloat16)

    grad_rows, distance = align(result_low, lengths, distance_cot, lambda: lax.axis_index("reg") * local_pairs)

    grad_result = cotangent.astype(jnp.float32) + grad_rows
    grad_second, grad_gain2, grad_shift2 = second_back(grad_result)
    grad_branch = grad_second.astype(jnp.bfloat16)
    grad_w_down = outer_rows(activated_low, grad_branch)
    grad_down_bias = jnp.sum(grad_branch.astype(jnp.float32), 0)
    (grad_inner,) = gelu_back(back_dot(grad_branch, w_down))
    grad_inner = grad_inner.astype(jnp.bfloat16)
    grad_w_in = outer_rows(normed_low, grad_inner)
    grad_in_bias = jnp.sum(grad_inner.astype(jnp.float32), 0)
    grad_normed = grad_second + back_dot(grad_inner, w_in)
    grad_first, grad_gain1, grad_shift1 = first_back(grad_normed)
    grad_attended = grad_first.astype(jnp.bfloat16)
    grad_w_out = outer_rows(context, grad_attended)
    grad_out_bias = jnp.sum(grad_attended.astype(jnp.float32), 0)
    grad_context = back_dot(grad_attended, w_out).astype(jnp.bfloat16).reshape(local_pairs, slot_rows, HEADS, HEAD_DIM)
    probs_again = jnp.exp(make_scores() - log_total)
    grad_probs = jnp.einsum("pqhd,pkhd->phqk", grad_context, values, preferred_element_type=jnp.float32)
    grad_values = jnp.einsum("phqk,pqhd->pkhd", probs_again.astype(jnp.bfloat16), grad_context, preferred_element_type=jnp.float32)
    grad_scores = probs_again * (grad_probs - jnp.sum(grad_probs * probs_again, -1, keepdims=True))
    grad_scores = grad_scores.astype(jnp.bfloat16)
    grad_queries = jnp.einsum("phqk,pkhd->pqhd", grad_scores, keys_all, preferred_element_type=jnp.float32) * score_scale
    grad_keys = jnp.einsum("phqk,pqhd->pkhd", grad_scores, queries, preferred_element_type=jnp.float32) * score_scale
    grad_packed = jnp.stack([grad_queries, grad_keys, grad_values], 2).reshape(local_rows, 3 * D).astype(jnp.bfloat16)
    grad_w_qkv = outer_rows(tokens, grad_packed)
    grad_bias_sum = jnp.sum(grad_packed.astype(jnp.float32), 0)
    grad_tokens = grad_first + back_dot(grad_packed, w_qkv)

    table = pack_table(grad_w_qkv, grad_w_out, grad_w_in, grad_w_down)
    singles = [grad_bias_sum[:D], grad_bias_sum[2 * D :], grad_out_bias, grad_gain1, grad_shift1, grad_down_bias, grad_gain2, grad_shift2]
    small = jnp.concatenate([jnp.stack(singles), grad_in_bias.reshape(4, D), jnp.zeros((4, D), f32)])
    table, small = sum_table(table, small, ndp)
    g_qkv, g_out, g_in, g_down = unpack_table(table)
    return (result_low, distance, grad_tokens, g_qkv, small[0], small[1], g_out, small[2], small[3], small[4],
            g_in, small[8:12].reshape(4 * D), g_down, small[5], small[6], small[7])


def solution(mesh):
    rows = P(("dp", "reg"), None)
    return jax.shard_map(
        functools.partial(on_device, mesh.shape["dp"]),
        mesh=mesh,
        in_specs=(rows, rows, P("dp"), P("dp", None)) + (P(),) * 13,
        out_specs=(rows, P(("dp", "reg")), rows) + (P(),) * 13,
        check_vma=False,
    )
```

time: 3850 us -> 563 us (0.15); the launches traced: 3800 us -> 552 us
  blocking collectives: 1410 us -> 0 us
  other arithmetic: 954 us -> 55.8 us
  local copies, waits for them, and re-layouts: 1040 us -> 162 us
  waiting for transfers between devices: 181 us -> 0 us
  Pallas kernels: 0 us -> 180 us
    psum x100 -> x0, blocking collectives: 1100 us -> none  [the longest x50 565 us: word_total_back(): return lax.psum(grad_total, 'reg')]
    reduce_sum x252 -> x0, other arithmetic: 341 us -> none  [the longest x100 156 us: half_first(): region_tot = jnp.sum(joined * word_scale[:, :, None], 1)]
    unnamed x2 -> x0, blocking collectives: 312 us -> none
    unnamed x189 -> x110, local copies, waits for them, and re-layouts: 265 us -> 22.8 us
    mul x152 -> x0, other arithmetic: 221 us -> none  [the longest x50 109 us: half_second(): transport = joined * region_scale[:, None, :] * word_scale[:, :, None]]
    dynamic_update_slice x150 -> x0, local copies, waits for them, and re-layouts: 195 us -> none  [on_device(): lax.scan(forward_step, (joint_mask, start_scale), None, length=ITERS)]
    add x51 -> x0, other arithmetic: 189 us -> none  [the longest x50 189 us: backward_step(): return ((grad_prev, grad_scale_prev, grad_kernel + more_kernel), None)]
    pallas_call x0 -> x6, Pallas kernels: none -> 180 us  [the longest x1 128 us: sum_table(): pl.pallas_call(kernel, out_shape=(jax.ShapeDtypeStruct((NBLK * BLK, COLS)...]
  transfers between devices with their start and end apart: 4 -> 0, of which waited for: 4 -> 0; matrix products, arithmetic and copies ran while one was open for 0% -> 0% of each run, Pallas kernels for 0% -> 0%
where the time goes in v1:
time: 563 us; the launch traced here: 552 us
  Pallas kernels  180 us (32%)
  local copies, waits for them, and re-layouts  162 us (29%)
  matrix products  152 us (27%)
  other arithmetic  55.8 us (10%)
    pallas_call x1, Pallas kernels, sum_table(): pl.pallas_call(kernel, out_shape=(jax.ShapeDtypeStruct((NBLK * BLK, COLS)...  128 us
    dot_general x4, matrix products, back_dot(): lax.dot_general(grad_in, weight_in, (((1,), (1,)), ((), ())), preferred_e...  41.6 us
    dot_general x1, matrix products, on_device(): jnp.dot(normed_low, w_in, preferred_element_type=jnp.float32) + in_bias  34 us
    pallas_call x4, Pallas kernels, widen(): pl.pallas_call(kernel, grid=grid, out_shape=jax.ShapeDtypeStruct(shape, f...  32.1 us
    dot_general x4, matrix products, outer_rows(): lax.dot_general(left_in, right_in, (((0,), (0,)), ((), ())), preferred_el...  25.9 us
    convert_element_type x2, local copies, waits for them, and re-layouts, on_device(): jnp.stack([grad_queries, grad_keys, grad_values], 2)  24.2 us
    unnamed x110, local copies, waits for them, and re-layouts  22.8 us
    pallas_call x1, Pallas kernels, align(): pl.pallas_call(k, out_shape=(jax.ShapeDtypeStruct((pairs * SLOT, D), f32)...  20.5 us

profile of v1, /device:TPU:0, one launch (start us, length us, event | category | flops | bytes accessed | tf_op | source)
XLA Modules:
  0.0 552.0 jit_solution(451965639349539598)
XLA Ops:
  10.7 14.1 %reshape.239 = bf16[5,192,3,12,64]{4,3,2,1,0:T(8,128)(2,1)} reshape(bf16[960,2304]{1,0:T(8,128)(2,1)} %add_convert_fusion.1) | data formatting | bytes 8847360 | tf_op jit(solution)/shard_map/reshape | solution.py:443
  24.8 8.5 %fusion.42 = (bf16[5,192,1,12,64]{4,3,2,1,0:T(8,128)(2,1)}, bf16[5,192,1,12,64]{4,3,2,1,0:T(8,128)(2,1)}, bf16[5,192,1,12,64]{4,3,2,1,0:T(8,128)(2,1)}) fusion(bf16[5,192,3,12,64]{4,3,2,1,0:T(8,128)(2,1)} %reshape.239), kind=kLoop, calls=%fused_computation.109 | loop fusion | bytes 8847360 | tf_op jit(solution)/shard_map/slice | solution.py:446
  78.0 34.0 %multiply_convert_fusion.1 = (bf16[960,3072]{1,0:T(8,128)(2,1)S(1)}, f32[960,3072]{1,0:T(8,128)}, f32[960,3072]{1,0:T(8,128)}) fusion(f32[3072]{0:T(1024)S(1)} %copy-done.42, bf16[768,3072]{1,0:T(8,128)(2,1)} %param.28, f32[960,768]{1,0:T(8,128)S(1)} %get-tuple-element.62, f32[768]{0:T(1024)S(1)} %copy-done.45, f32[768]{0:T(1024)S(1)} %copy-done.33, ...), kind=kOutput, calls=%fused_computation.10 | convolution fusion | flops 4728176640 | bytes 37185024 | tf_op jit(solution)/shard_map/dot_general | solution.py:464
  120.5 20.5 %shard_map.288 = (f32[960,768]{1,0:T(8,128)}, f32[5]{0:T(128)}) custom-call(bf16[960,768]{1,0:T(8,128)(2,1)} %add_convert_fusion.2.rows_ref, s32[20,2]{1,0:T(8,128)} %copy.69.len_ref, f32[20]{0:T(128)} %dcot_ref.1), custom_call_target="tpu_custom_call" | custom-call | tf_op jit(solution)/shard_map/pallas_call | solution.py:413
  149.9 16.6 %convert_reduce_fusion = (f32[3072]{0:T(1024)}, bf16[960,3072]{1,0:T(8,128)(2,1)}) fusion(f32[960,3072]{1,0:T(8,128)} %get-tuple-element.51, f32[960,3072]{1,0:T(8,128)} %get-tuple-element.63, f32[3072]{0:T(1024)S(1)} %copy-done.42, bf16[960,768]{1,0:T(8,128)(2,1)S(1)} %get-tuple-element.41, bf16[3072,768]{1,0:T(8,128)(2,1)} %param.30), kind=kOutput, calls=%fused_computation.4 | convolution fusion | flops 4579980288 | bytes 35708928 | tf_op jit(solution)/shard_map/dot_general | solution.py:429
  166.5 9.5 %convolution_convert_fusion.1 = bf16[3072,768]{1,0:T(8,128)(2,1)} fusion(bf16[960,3072]{1,0:T(8,128)(2,1)} %copy-done.47, bf16[960,768]{1,0:T(8,128)(2,1)S(1)} %get-tuple-element.41), kind=kOutput, calls=%fused_computation.35 | convolution fusion | flops 4532207616 | bytes 12091392 | tf_op jit(solution)/shard_map/dot_general | solution.py:425
  184.2 13.5 %multiply_reduce_fusion.2 = (f32[768]{0:T(1024)}, f32[960]{0:T(1024)}, f32[768]{0:T(1024)}, f32[960,768]{1,0:T(8,128)}) fusion(f32[960,768]{1,0:T(8,128)} %copy-done.8, f32[960]{0:T(1024)} %copy-done.26, f32[960]{0:T(1024)S(1)} %broadcast_multiply_fusion.1, f32[768]{0:T(1024)} %param.26, bf16[960,3072]{1,0:T(8,128)(2,1)} %get-tuple-element.39, ...), kind=kOutput, calls=%fused_computation.46 | convolution fusion | flops 4537218048 | bytes 19488768 | tf_op jit(solution)/shard_map/dot_general | solution.py:429
  197.7 9.8 %convolution_convert_fusion = bf16[768,3072]{1,0:T(8,128)(2,1)} fusion(bf16[960,3072]{1,0:T(8,128)(2,1)} %get-tuple-element.39, f32[960,768]{1,0:T(8,128)S(1)} %copy-done.9, f32[768]{0:T(1024)S(1)} %copy-done.46, f32[768]{0:T(1024)S(1)} %copy-done.34, f32[960]{0:T(1024)S(1)} %copy-done.27, f32[960]{0:T(1024)S(1)} %broadcast_multiply_fusion.1), kind=kOutput, calls=%fused_computation.34 | convolution fusion | flops 4535894016 | bytes 13579776 | tf_op jit(solution)/shard_map/dot_general | solution.py:425
  207.5 11.8 %reshape.229 = bf16[768,6,2,256]{3,2,1,0:T(2,128)(2,1)} reshape(bf16[768,3072]{1,0:T(8,128)(2,1)} %convolution_convert_fusion) | data formatting | bytes 9437184 | tf_op jit(solution)/shard_map/reshape | solution.py:310
  233.2 10.2 %reshape.227 = bf16[6,512,3,256]{1,0,3,2:T(8,128)(2,1)} reshape(bf16[3072,768]{0,1:T(8,128)(2,1)} %copy.77) | data formatting | bytes 9437184 | tf_op jit(solution)/shard_map/reshape | solution.py:309
  243.5 8.6 %copy.78 = bf16[6,3,512,256]{3,2,1,0:T(8,128)(2,1)} copy(bf16[6,3,512,256]{2,0,3,1:T(8,128)(2,1)} %bitcast.87) | data formatting | bytes 9437184 | tf_op jit(solution)/shard_map/transpose | solution.py:309
  252.0 8.4 %pad_maximum_fusion.1 = bf16[6,2,1536,256]{3,2,0,1:T(8,128)(2,1)} fusion(bf16[6,1,1536,256]{3,2,0,1:T(8,128)(2,1)} %bitcast.91, bf16[6,1,1536,256]{3,2,0,1:T(8,128)(2,1)} %bitcast.92), kind=kLoop, calls=%fused_computation.28 | loop fusion | flops 4718592 | bytes 18874368 | tf_op jit(solution)/shard_map/concatenate | solution.py:311
  260.4 8.0 %copy.80 = bf16[6,2,1536,256]{3,2,1,0:T(8,128)(2,1)} copy(bf16[6,2,1536,256]{3,2,0,1:T(8,128)(2,1)} %pad_maximum_fusion.1) | data formatting | bytes 18874368 | tf_op jit(solution)/shard_map/concatenate | solution.py:311
  280.4 9.1 %fusion.15 = bf16[5,192,1,12,64]{1,4,3,0,2:T(8,128)(2,1)} fusion(bf16[5,192,12,64]{1,3,2,0:T(8,128)(2,1)} %copy.71, f32[5,12,192]{2,1,0:T(8,128)} %log_add_fusion, f32[5,12,192,192]{2,3,1,0:T(8,128)} %copy-done.1, pred[5,192]{1,0:T(8,128)(4,1)S(1)} %copy-done.22), kind=kOutput, calls=%fused_computation.62 | convolution fusion | flops 291962880 | bytes 11843520 | tf_op jit(solution)/shard_map/phqk,pqhd->pkhd/dot_general | solution.py:490
  289.5 13.8 %multiply_reduce_fusion = (f32[5,12,192]{2,1,0:T(8,128)S(1)}, f32[5,12,192,192]{2,3,1,0:T(8,128)}) fusion(f32[5,12,192]{2,1,0:T(8,128)S(1)} %copy-done.20, f32[5,12,192,192]{2,3,1,0:T(8,128)} %copy-done.1, pred[5,192]{1,0:T(8,128)(4,1)S(1)} %copy-done.22, bf16[5,192,12,64]{1,3,2,0:T(8,128)(2,1)} %copy.71, bf16[5,192,1,12,64]{1,4,3,0,2:T(8,128)(2,1)S(1)} %copy-done.13), kind=kOutput, calls=%fused_computation.7 | convolution fusion | flops 294163200 | bytes 20736960 | tf_op jit(solution)/shard_map/pqhd,pkhd->phqk/dot_general | solution.py:489
  303.3 7.4 %multiply_convert_fusion = bf16[5,12,192,192]{2,3,1,0:T(8,128)(2,1)S(1)} fusion(f32[5,12,192,192]{2,3,1,0:T(8,128)} %get-tuple-element.68, f32[5,12,192]{2,1,0:T(8,128)S(1)} %get-tuple-element.67, f32[5,12,192]{2,1,0:T(8,128)S(1)} %copy-done.20, f32[5,12,192,192]{2,3,1,0:T(8,128)S(1)} %bitcast.85, pred[5,192]{1,0:T(8,128)(4,1)S(1)} %copy-done.22), kind=kLoop, calls=%fused_computation.6 | loop fusion | flops 13271040 | bytes 22211520 | tf_op jit(solution)/shard_map/convert_element_type | solution.py:492
  324.8 11.4 %copy.76 = bf16[5,192,3,12,64]{1,0,4,3,2:T(8,128)(2,1)} copy(bf16[5,192,3,12,64]{1,4,3,0,2:T(8,128)(2,1)} %get-tuple-element.45) | data formatting | bytes 8847360 | tf_op jit(solution)/shard_map/convert_element_type | solution.py:495
  336.2 12.8 %convert_element_type.96 = bf16[960,2304]{0,1:T(8,128)(2,1)} reshape(bf16[5,192,3,12,64]{1,0,4,3,2:T(8,128)(2,1)} %copy.76) | data formatting | bytes 8847360 | tf_op jit(solution)/shard_map/convert_element_type | solution.py:495
  349.1 9.0 %add_add_fusion.4 = f32[960,768]{1,0:T(8,128)} fusion(f32[960,768]{1,0:T(8,128)} %copy-done.11, bf16[960,2304]{0,1:T(8,128)(2,1)} %convert_element_type.96, bf16[768,2304]{1,0:T(8,128)(2,1)S(1)} %copy-done, f32[960]{0:T(1024)S(1)} %copy-done.30), kind=kOutput, calls=%fused_computation.57 | convolution fusion | flops 3398860800 | bytes 13864704 | tf_op jit(solution)/shard_map/dot_general | solution.py:429
  371.3 17.6 %pad_maximum_fusion.table_in = bf16[27648,256]{1,0:T(8,128)(2,1)} fusion(bf16[9216,256]{1,0:T(8,128)(2,1)} %bitcast.88, bf16[18432,256]{1,0:T(8,128)(2,1)} %bitcast.86), kind=kLoop, calls=%fused_computation.1 | loop fusion | flops 28311552 | bytes 28311552 | tf_op jit(solution)/shard_map/concatenate | solution.py:313
  388.9 127.7 %sum_table.1 = (bf16[27648,256]{1,0:T(8,128)(2,1)}, f32[16,768]{1,0:T(8,128)}) custom-call(bf16[27648,256]{1,0:T(8,128)(2,1)} %pad_maximum_fusion.table_in, f32[16,768]{1,0:T(8,128)} %concatenate.20.small_ref), custom_call_target="tpu_custom_call" | custom-call | tf_op jit(solution)/shard_map/sum_table/pallas_call | solution.py:275
  523.0 7.4 %widen.4 = f32[768,2304]{1,0:T(8,128)} custom-call(bf16[27648,256]{1,0:T(8,128)(2,1)} %get-tuple-element.22.a), custom_call_target="tpu_custom_call" | custom-call | tf_op jit(solution)/shard_map/widen/pallas_call | solution.py:290
  530.4 12.0 %widen.7 = f32[3072,768]{1,0:T(8,128)} custom-call(bf16[27648,256]{1,0:T(8,128)(2,1)} %get-tuple-element.22.a), custom_call_target="tpu_custom_call" | custom-call | tf_op jit(solution)/shard_map/widen/pallas_call | solution.py:290
  542.3 9.4 %widen.6 = f32[768,3072]{1,0:T(8,128)} custom-call(bf16[27648,256]{1,0:T(8,128)(2,1)} %get-tuple-element.22.a), custom_call_target="tpu_custom_call" | custom-call | tf_op jit(solution)/shard_map/widen/pallas_call | solution.py:290
  (172 shorter events, 139.0 us)
Async XLA Ops:
  1.7 59.3 %copy-start.21 = (pred[5,192]{1,0:T(8,128)(4,1)}, pred[5,192]{1,0:T(8,128)(4,1)S(1)}, u32[]{:S(2)}) copy-start(pred[5,192]{1,0:T(8,128)(4,1)S(1)} %fusion.29) | copy-start | bytes 2884
  64.1 8.4 %copy-start.43 = (f32[768]{0:T(1024)S(1)}, f32[768]{0:T(1024)}, u32[]{:S(2)}) copy-start(f32[768]{0:T(1024)} %param.25) | copy-start | bytes 9220
  72.5 39.6 %slice-start.3 = ((s8[4718592]{0:T(1024)(128)(4,1)}), s8[4194304]{0:T(1024)(128)(4,1)S(1)}, s32[]{:S(2)}) async-start(s8[4718592]{0:T(1024)(128)(4,1)} %bitcast.93), calls=%async_computation.3 | async-start | bytes 8388608
  76.5 35.6 %copy-start.8 = (f32[960,768]{1,0:T(8,128)}, f32[960,768]{1,0:T(8,128)S(1)}, u32[]{:S(2)}) copy-start(f32[960,768]{1,0:T(8,128)S(1)} %get-tuple-element.62) | copy-start | bytes 8847364
  78.0 34.1 %copy-start.26 = (f32[960]{0:T(1024)}, f32[960]{0:T(1024)S(1)}, u32[]{:S(2)}) copy-start(f32[960]{0:T(1024)S(1)} %fusion.30) | copy-start | bytes 11524
  78.0 34.1 %slice-start.4 = ((s8[4718592]{0:T(1024)(128)(4,1)}), s8[524288]{0:T(1024)(128)(4,1)S(1)}, s32[]{:S(2)}) async-start(s8[4718592]{0:T(1024)(128)(4,1)} %bitcast.93), calls=%async_computation.4 | async-start | bytes 1048576
  78.0 34.1 %copy-start.44 = (f32[768]{0:T(1024)S(1)}, f32[768]{0:T(1024)}, u32[]{:S(2)}) copy-start(f32[768]{0:T(1024)} %param.31) | copy-start | bytes 9220
  112.1 6.8 %copy-start.25 = (f32[768]{0:T(1024)S(1)}, f32[768]{0:T(1024)}, u32[]{:S(2)}) copy-start(f32[768]{0:T(1024)} %param.32) | copy-start | bytes 9220
  148.0 18.5 %copy-start.31 = (f32[960]{0:T(1024)}, f32[960]{0:T(1024)S(1)}, u32[]{:S(2)}) copy-start(f32[960]{0:T(1024)S(1)} %negate_multiply_fusion.2) | copy-start | bytes 11524
  184.1 13.6 %copy-start.9 = (f32[960,768]{1,0:T(8,128)S(1)}, f32[960,768]{1,0:T(8,128)}, u32[]{:S(2)}) copy-start(f32[960,768]{1,0:T(8,128)} %copy-done.8) | copy-start | bytes 8847364
  184.2 13.6 %copy-start.27 = (f32[960]{0:T(1024)S(1)}, f32[960]{0:T(1024)}, u32[]{:S(2)}) copy-start(f32[960]{0:T(1024)} %copy-done.26) | copy-start | bytes 11524
  184.2 13.5 %copy-start.34 = (f32[768]{0:T(1024)S(1)}, f32[768]{0:T(1024)}, u32[]{:S(2)}) copy-start(f32[768]{0:T(1024)} %param.26) | copy-start | bytes 9220
  184.2 13.5 %copy-start.46 = (f32[768]{0:T(1024)S(1)}, f32[768]{0:T(1024)}, u32[]{:S(2)}) copy-start(f32[768]{0:T(1024)} %param.27) | copy-start | bytes 9220
  268.4 11.9 %copy-start.22 = (pred[5,192]{1,0:T(8,128)(4,1)S(1)}, pred[5,192]{1,0:T(8,128)(4,1)}, u32[]{:S(2)}) copy-start(pred[5,192]{1,0:T(8,128)(4,1)} %copy-done.21) | copy-start | bytes 2884
  280.3 9.2 %copy-start.13 = (bf16[5,192,1,12,64]{1,4,3,0,2:T(8,128)(2,1)S(1)}, bf16[5,192,1,12,64]{1,4,3,0,2:T(8,128)(2,1)}, u32[]{:S(2)}) copy-start(bf16[5,192,1,12,64]{1,4,3,0,2:T(8,128)(2,1)} %copy.90) | copy-start | bytes 4423684
  280.3 9.2 %copy-start.20 = (f32[5,12,192]{2,1,0:T(8,128)S(1)}, f32[5,12,192]{2,1,0:T(8,128)}, u32[]{:S(2)}) copy-start(f32[5,12,192]{2,1,0:T(8,128)} %log_add_fusion) | copy-start | bytes 138244
  280.4 23.0 %slice-start = ((s8[11796480]{0:T(1024)(128)(4,1)}), s8[4194304]{0:T(1024)(128)(4,1)S(1)}, s32[]{:S(2)}) async-start(s8[11796480]{0:T(1024)(128)(4,1)} %bitcast.84), calls=%async_computation | async-start | bytes 8388608
  280.4 22.9 %slice-start.1 = ((s8[11796480]{0:T(1024)(128)(4,1)}), s8[4194304]{0:T(1024)(128)(4,1)S(1)}, s32[]{:S(2)}) async-start(s8[11796480]{0:T(1024)(128)(4,1)} %bitcast.84), calls=%async_computation.1 | async-start | bytes 8388608
  289.5 13.8 %slice-start.2 = ((s8[11796480]{0:T(1024)(128)(4,1)}), s8[3407872]{0:T(1024)(128)(4,1)S(1)}, s32[]{:S(2)}) async-start(s8[11796480]{0:T(1024)(128)(4,1)} %bitcast.84), calls=%async_computation.2 | async-start | bytes 6815744
  303.3 7.5 %copy-start.5 = (bf16[5,192,1,12,64]{1,4,3,0,2:T(8,128)(2,1)S(1)}, bf16[5,192,1,12,64]{1,4,3,0,2:T(8,128)(2,1)}, u32[]{:S(2)}) copy-start(bf16[5,192,1,12,64]{1,4,3,0,2:T(8,128)(2,1)} %copy.91) | copy-start | bytes 4423684
  314.4 7.7 %copy-start.32 = (f32[1,768]{1,0:T(1,128)S(1)}, f32[1,768]{1,0:T(1,128)}, u32[]{:S(2)}) copy-start(f32[1,768]{1,0:T(1,128)} %reshape.235) | copy-start | bytes 9220
  336.2 12.8 %copy-start.30 = (f32[960]{0:T(1024)S(1)}, f32[960]{0:T(1024)}, u32[]{:S(2)}) copy-start(f32[960]{0:T(1024)} %copy-done.29) | copy-start | bytes 11524
  349.1 9.0 %copy-start.15 = (bf16[960,2304]{0,1:T(8,128)(2,1)S(1)}, bf16[960,2304]{0,1:T(8,128)(2,1)}, u32[]{:S(2)}) copy-start(bf16[960,2304]{0,1:T(8,128)(2,1)} %convert_element_type.96) | copy-start | bytes 13271044
  349.1 9.0 %copy-start.40 = (bf16[960,768]{1,0:T(8,128)(2,1)S(1)}, bf16[960,768]{1,0:T(8,128)(2,1)}, u32[]{:S(2)}) copy-start(bf16[960,768]{1,0:T(8,128)(2,1)} %param.17) | copy-start | bytes 4423684
  (29 other events, 124.1 us)
